TPU v7x, 512 devices: a whole 4x8x8 slice. The times are simulated.
512 devices in a mesh: row: 8 (over y), col: 32 (over z, x), cores: 2 (over core).
Axes of the slice: x: 4, y: 8, z: 8, core: 2. Of those that a mesh axis runs over, the one named last changes fastest.
Arguments:
- root_rhs: bfloat16 [20480, 256], P(('col', 'cores')), may hold values from -6 to 6
- root_inverse: bfloat16 [20480, 20480], P(('col', 'cores'), 'row'), as said below
- child_rhs: bfloat16 [2, 10240, 256], P('cores', 'col'), may hold values from -6 to 6
- child_inverse: bfloat16 [2, 10240, 10240], P('cores', 'col', 'row'), as said below
- coupling: bfloat16 [2, 20480, 10240], P('cores', 'row', 'col'), may hold values from -0.0390625 to 0.0390625
- block_map: int32 [2, 160], replicated, may hold values from 0 to 159, as said below
- block_count: int32 [2], replicated, may hold values from 80 to 160, as said below
Outputs:
- root_solution: bfloat16 [20480, 256], P(('row', 'col', 'cores'))
- child_solution: bfloat16 [2, 10240, 256], P('cores', ('row', 'col'))
Inputs may be any that keep to these rules, and one draw needn't show every extreme that they name: `root_inverse`: entries whose row index is below the column index are zero. `child_inverse`: entries whose row index is below the column index are zero. `block_map`: the slots of a child form aligned groups of 20; range p holds blocks p * 20 to p * 20 + 19. In each group at most 3 slots name blocks of one range, some range is named exactly 3 times, and slots of one group naming one range name different blocks. Slots k of child f with k >= block_count[f] are padding. Some child has 160 live slots.
All inputs are finite; a program needn't handle non-finite values.
Results may differ from a plain program's by a relative error of at most 0.0054.
Values may be sent and summed in bfloat16 or wider, within the bound.
A program may use at most 64 MiB of HBM per device.

v0:
```python
import jax
import jax.numpy as jnp
from jax import lax
from jax.sharding import PartitionSpec as P

BLOCK = 128


def contract_rows(matrix, right):
    return lax.dot_general(
        matrix, right, (((0,), (0,)), ((), ())), preferred_element_type=jnp.float32
    )


def per_device(root_rhs, root_inverse, child_rhs, child_inverse, coupling, block_map, block_count):
    load_cases = root_rhs.shape[1]
    columns = root_inverse
    root_solution = lax.psum_scatter(
        contract_rows(columns, root_rhs), ("col", "cores"), scatter_dimension=0, tiled=True
    ).astype(jnp.bfloat16)
    groups = lax.axis_size("row")
    row_index = lax.axis_index("row")
    core_index = lax.axis_index("cores")
    slots_total = block_map.shape[1]
    group_size = slots_total // groups
    front_map = lax.dynamic_index_in_dim(block_map, core_index, 0, keepdims=False)
    front_count = lax.dynamic_index_in_dim(block_count, core_index, 0, keepdims=False)
    slot_ids = row_index * group_size + jnp.arange(group_size, dtype=jnp.int32)
    whole_solution = lax.all_gather(root_solution, ("row", "col", "cores"), axis=0, tiled=True)
    all_blocks = whole_solution.reshape(-1, BLOCK, load_cases)
    my_blocks = lax.dynamic_slice_in_dim(front_map, row_index * group_size, group_size)
    picked = jnp.take(all_blocks, my_blocks, axis=0)
    alive_slots = slot_ids < front_count
    picked = jnp.where(alive_slots[:, None, None], picked, jnp.zeros((), jnp.bfloat16))
    picked = picked.reshape(group_size * BLOCK, load_cases)
    coupled = contract_rows(coupling[0], picked)
    coupled = lax.psum(coupled, "row")
    reduced = (child_rhs[0].astype(jnp.float32) - coupled).astype(jnp.bfloat16)
    columns = child_inverse[0]
    child_solution = lax.psum_scatter(
        contract_rows(columns, reduced), "col", scatter_dimension=0, tiled=True
    ).astype(jnp.bfloat16)
    return (root_solution, child_solution[None])


def solution(mesh):
    in_specs = (
        P(("col", "cores"), None),
        P(("col", "cores"), "row"),
        P("cores", "col", None),
        P("cores", "col", "row"),
        P("cores", "row", "col"),
        P(),
        P(),
    )
    out_specs = (P(("row", "col", "cores"), None), P("cores", ("row", "col"), None))
    return jax.shard_map(
        per_device, mesh=mesh, in_specs=in_specs, out_specs=out_specs, check_vma=False
    )
```

profile of v0, /device:TPU:40, one launch (start us, length us, event | category | flops | bytes accessed | tf_op | source)
XLA Modules:
  0.0 615.1 jit_solution(10541471222368096795)
XLA Ops:
  7.2 0.0 copy-start
  7.2 0.0 reduce-scatter.9.cloned.1.call-start
  7.2 0.0 copy-done
  7.2 3.3 fusion.10
  10.5 0.0 copy-start.4
  10.5 0.0 copy-start.2
  10.6 0.0 reduce-scatter.9.cloned.1.call-update
  10.6 0.0 all-gather.2.cloned.1.call-start
  10.6 157.1 %reduce-scatter.9.cloned.1.call-done = f32[40,256]{1,0:T(8,128)} async-done(((f32[2560,256]{1,0:T(8,128)}), f32[40,256]{1,0:T(8,128)}) %reduce-scatter.9.cloned.1.call-update) | async-done | bytes 40976
  167.7 1.4 convert_element_type.15
  169.1 0.0 all-gather.2.cloned.1.call-update
  169.1 0.0 all-reduce.3.cloned.1.call-start
  169.2 0.0 copy-done.4
  169.2 0.6 dynamic_slice.13
  169.8 0.0 copy-done.2
  169.8 0.1 fusion.9
  169.8 0.7 compare_and_fusion
  170.6 128.7 %all-gather.2.cloned.1.call-done = bf16[20480,256]{1,0:T(8,128)(2,1)} async-done(((bf16[40,256]{1,0:T(8,128)(2,1)}), bf16[20480,256]{1,0:T(8,128)(2,1)}) %all-gather.2.cloned.1.call-update) | async-done | bytes 10485776 | tf_op jit(solution)/shard_map/all_gather | solution.py:29
  299.3 4.6 gather_fusion
  303.9 0.0 copy-start.3
  303.9 0.3 select_select_fusion
  304.2 1.2 copy-done.3
  305.3 0.0 copy-start.1
  305.3 1.3 fusion.2
  306.6 0.0 all-reduce.3.cloned.1.call-update
  306.6 0.0 reduce-scatter.7.cloned.1.call-start
  306.7 73.4 %all-reduce.3.cloned.1.call-done = f32[320,256]{1,0:T(8,128)} async-done(((f32[320,256]{1,0:T(8,128)}), f32[320,256]{1,0:T(8,128)}) %all-reduce.3.cloned.1.call-update) | async-done | bytes 327696 | tf_op jit(solution)/shard_map/psum | solution.py:37
  380.1 0.0 copy-done.1
  380.1 1.8 convolution_bitcast_fusion
  381.9 1.5 copy.11
  383.4 0.0 reduce-scatter.7.cloned.1.call-update
  383.4 223.6 %reduce-scatter.7.cloned.1.call-done = f32[40,256]{1,0:T(8,128)} async-done(((f32[1280,256]{1,0:T(8,128)}), f32[40,256]{1,0:T(8,128)}) %reduce-scatter.7.cloned.1.call-update) | async-done | bytes 40976
  607.0 0.9 copy.12
  607.9 0.7 copy.10
  (1 shorter events, 0.0 us)
Async XLA Ops:
  7.2 0.1 copy-start
  7.2 160.5 %reduce-scatter.9.cloned.1.call-start = ((), (), s32[]{:S(2)}) async-start(), calls=%async_computation.5 | async-start | bytes 2662400
  10.5 158.6 %copy-start.4 = (s32[2]{0:T(128)S(1)}, s32[2]{0:T(128)}, u32[]{:S(2)}) copy-start(s32[2]{0:T(128)} %param.13) | copy-start | bytes 28
  10.5 159.2 %copy-start.2 = (s32[2,160]{1,0:T(2,128)S(1)}, s32[2,160]{1,0:T(2,128)}, u32[]{:S(2)}) copy-start(s32[2,160]{1,0:T(2,128)} %param.12) | copy-start | bytes 3844
  10.6 288.7 %all-gather.2.cloned.1.call-start = ((), (), s32[]{:S(2)}) async-start(), calls=%async_computation.2 | async-start | bytes 10506240 | tf_op jit(solution)/shard_map/all_gather | solution.py:29
  169.1 211.0 %all-reduce.3.cloned.1.call-start = ((), (), s32[]{:S(2)}) async-start(), calls=%async_computation.3 | async-start | bytes 655360 | tf_op jit(solution)/shard_map/psum | solution.py:37
  303.9 1.4 copy-start.3
  305.3 74.8 %copy-start.1 = (bf16[1,320,256]{2,1,0:T(8,128)(2,1)S(1)}, bf16[1,320,256]{2,1,0:T(8,128)(2,1)}, u32[]{:S(2)}) copy-start(bf16[1,320,256]{2,1,0:T(8,128)(2,1)} %param.9) | copy-start | bytes 491524
  306.6 300.4 %reduce-scatter.7.cloned.1.call-start = ((), (), s32[]{:S(2)}) async-start(), calls=%async_computation.4 | async-start | bytes 1351680
Sparse Core Ops, SparseCore 0:
  12.7 154.9 reduce-scatter.8
  173.6 125.6 all-gather.1
  306.8 73.3 all-reduce.2
  384.4 222.5 reduce-scatter.6
where the time goes:
time: 616 us; the launch traced here: 615 us
  waiting for transfers between devices  583 us (95%)
  between operations  13.8 us (2%)
  local copies, waits for them, and re-layouts  9.45 us (2%)
  matrix products  6.39 us (1%)
    unnamed x6, waiting for transfers between devices  381 us
    all_gather x1, waiting for transfers between devices, per_device(): lax.all_gather(root_solution, ('row', 'col', 'cores'), axis=0, tiled=True)  129 us
    psum x1, waiting for transfers between devices, per_device(): coupled = lax.psum(coupled, 'row')  73.4 us
  transfers between devices with their start and end apart: 4, of which 4 were waited for; matrix products, arithmetic and copies ran while one was open for 0% of the time, Pallas kernels for 0%

commit v1 on v0

v1 whole, which is shorter than its diff:
```python
import functools

import jax
import jax.numpy as jnp
from jax import lax
from jax.experimental import pallas as pl
from jax.experimental.pallas import tpu as pltpu
from jax.sharding import PartitionSpec as P

BLOCK = 128
CAP = 3
GRID = {32: (4, 8), 4: (2, 2)}
MESH = pl.DeviceIdType.MESH
BF = jnp.bfloat16
F32 = jnp.float32


class Sizes:
    def __init__(self, mesh, root_rhs, root_inverse, child_inverse, coupling, block_map):
        self.NY = mesh.shape["row"]
        self.NX, self.NZ = GRID[mesh.shape["col"]]
        self.Q = self.NX * self.NZ
        self.S1, self.C = root_rhs.shape
        self.T1 = root_inverse.shape[1]
        self.NB = self.T1 // BLOCK
        self.HB = self.NB // 2
        self.CB = 2
        self.NCH = self.HB // self.CB
        self.S3, self.T3 = child_inverse.shape[1:]
        self.U = coupling.shape[1]
        self.G = self.U // BLOCK
        self.CY = self.C // self.NY
        self.TO = self.T1 // (2 * self.Q)
        self.TC = self.T3 // self.Q
        self.TZ = self.T1 // self.NZ
        starts = [self.TZ * z // BLOCK for z in range(self.NZ)]
        ends = [-(-self.TZ * (z + 1) // BLOCK) for z in range(self.NZ)]
        self.SPAN = max(e - s for s, e in zip(starts, ends))


def far_first(n):
    return sorted(range(1, n), key=lambda d: (-min(d, n - d), d))


def kernel(
    sz, rrhs, rinv, crhs, cinv, coup, bmap, bcnt, rout, cout, *,
    rinv_v, coup_v, cinv_v, cit, rhs_t, crhs_t, cs, cr, own, xs, xr, zacc, zs, zr, sol,
    ysd, yrc, gath, lhs, ycs, y1s, ycr, red, o1, o2, ot, p5f, p5s, p5r, z5s, z5r, sel, pos,
    lsem, csem, xsem, zsem, c2sem, ysem, o1sem, o2sem, agx, agu, agd, y1sem, y2sem, p5sem, z5sem,
):
    NX, NZ, NY, NCH, CB, HB, NB, G = sz.NX, sz.NZ, sz.NY, sz.NCH, sz.CB, sz.HB, sz.NB, sz.G
    r, c, k = lax.axis_index("row"), lax.axis_index("col"), lax.axis_index("cores")
    z, x = c // NX, lax.rem(c, NX)

    def xd(d):
        return lax.rem(x + d + NX, NX)

    def zd(d):
        return lax.rem(z + d + NZ, NZ)

    def yd(d):
        return lax.rem(r + d + NY, NY)

    def dev_x(d):
        return (r, z * NX + xd(d), k)

    def dev_z(d):
        return (r, zd(d) * NX + x, k)

    def dev_y(d):
        return (yd(d), c, k)

    dev_c = (r, c, 1 - k)
    sent = []

    def send(src, dst, sem, idx, dev):
        cp = pltpu.make_async_remote_copy(
            src_ref=src, dst_ref=dst, send_sem=sem.at[(0,) + idx], recv_sem=sem.at[(1,) + idx],
            device_id=dev, device_id_type=MESH,
        )
        cp.start()
        sent.append(cp)

    def arrived(ref, sem, idx):
        pltpu.make_async_remote_copy(
            src_ref=ref, dst_ref=ref, send_sem=sem.at[(0,) + idx], recv_sem=sem.at[(1,) + idx],
            device_id=dev_c, device_id_type=MESH,
        ).wait_recv()

    barrier = pltpu.get_barrier_semaphore()
    peers = (
        [dev_c]
        + [dev_x(d) for d in range(1, NX)]
        + [dev_z(d) for d in range(1, NZ)]
        + [dev_y(d) for d in range(1, NY)]
    )
    for dev in peers:
        pl.semaphore_signal(barrier, inc=1, device_id=dev, device_id_type=MESH)

    half = HB * BLOCK
    loads = [
        pltpu.make_async_copy(
            rinv.at[:, pl.ds(pl.multiple_of((1 - k) * half, BLOCK), half)],
            rinv_v.at[:, pl.ds(pl.multiple_of((1 - k) * half, BLOCK), half)], lsem.at[0]),
        pltpu.make_async_copy(
            rinv.at[:, pl.ds(pl.multiple_of(k * half, BLOCK), half)],
            rinv_v.at[:, pl.ds(pl.multiple_of(k * half, BLOCK), half)], lsem.at[1]),
        pltpu.make_async_copy(cinv.at[0], cinv_v, lsem.at[2]),
        pltpu.make_async_copy(coup.at[0], coup_v, lsem.at[3]),
    ]
    for cp in loads:
        cp.start()
    rhs_t[...] = rrhs[...].astype(F32).T.astype(BF)

    def partial(which, dst, ch):
        off = pl.multiple_of(which * half + ch * CB * BLOCK, BLOCK)
        v = jnp.dot(rhs_t[...], rinv_v[:, pl.ds(off, CB * BLOCK)], preferred_element_type=F32)
        for b in range(CB):
            dst[ch, :, b] = v[:, b * BLOCK:(b + 1) * BLOCK].reshape(sz.Q, 8, BLOCK)

    loads[0].wait()
    for ch in range(NCH):
        partial(1 - k, cs, ch)
        if ch == 0:
            pl.semaphore_wait(barrier, len(peers))
        send(cs.at[ch], cr.at[ch], csem, (ch,), dev_c)
    loads[1].wait()
    for ch in range(NCH):
        partial(k, own, ch)

    mine_x = pl.ds(x * NZ, NZ)
    for ch in range(NCH):
        arrived(cr.at[ch], csem, (ch,))
        for d in range(1, NX):
            rows = pl.ds(xd(d) * NZ, NZ)
            xs[ch, d] = (own[ch, rows] + cr[ch, rows]).astype(BF)
            send(xs.at[ch, d], xr.at[ch, d], xsem, (ch, d), dev_x(d))

    def choose(t, _):
        cnt = jnp.int32(0)
        got = [jnp.int32(0)] * CAP
        for s in range(G):
            b = bmap[k, t * G + s] - r * NB
            inside = jnp.logical_and(b >= 0, b < NB)
            for j in range(CAP):
                got[j] = jnp.where(jnp.logical_and(inside, cnt == j), b, got[j])
            cnt = cnt + jnp.where(inside, 1, 0)
        for j in range(CAP):
            sel[t * CAP + j] = got[j]
        return 0

    lax.fori_loop(0, NY, choose, 0)
    ranges = [lax.div(bmap[k, r * G + s], jnp.int32(NB)) for s in range(G)]
    for s in range(G):
        rank = jnp.int32(0)
        for e in range(s):
            rank = rank + jnp.where(ranges[e] == ranges[s], 1, 0)
        pos[s] = ranges[s] * CAP + jnp.minimum(rank, CAP - 1)

    for ch in range(NCH):
        acc = own[ch, mine_x] + cr[ch, mine_x]
        for d in range(1, NX):
            arrived(xr.at[ch, d], xsem, (ch, d))
            acc = acc + xr[ch, d].astype(F32)
        zacc[ch] = acc
        zs[ch] = acc.astype(BF)
        for d in far_first(NZ):
            send(zs.at[ch, zd(d)], zr.at[ch, d], zsem, (ch, d), dev_z(d))

    loads[2].wait()
    for j in range(sz.T3 // BLOCK):
        cols = slice(j * BLOCK, (j + 1) * BLOCK)
        cit[cols, :] = cinv_v[:, cols].astype(F32).T.astype(BF)
    crhs_t[...] = crhs[0].astype(F32).T

    for ch in range(NCH):
        acc = zacc[ch, z]
        for d in range(1, NZ):
            arrived(zr.at[ch, d], zsem, (ch, d))
            acc = acc + zr[ch, d].astype(F32)
        sol[pl.ds(k * HB + ch * CB, CB)] = acc.astype(BF)
    mine = pl.ds(k * HB, HB)
    send(sol.at[mine], sol.at[mine], c2sem, (0,), dev_c)
    arrived(sol.at[pl.ds((1 - k) * HB, HB)], c2sem, (0,))

    for d in far_first(NY) + [0]:
        t = yd(d)
        for j in range(CAP):
            v = sol[sel[t * CAP + j]]
            if d:
                ysd[d, j] = v
            else:
                yrc[r, j] = v
        if d:
            send(ysd.at[d], yrc.at[r], ysem, (d,), dev_y(d))
    def first_block(zz):
        return (sz.TZ * zz) // BLOCK

    for d in far_first(NZ):
        send(sol.at[pl.ds(first_block(zd(d)), sz.SPAN)], o1.at[z], o1sem, (d,), dev_z(d))
    o1[z] = sol[pl.ds(first_block(z), sz.SPAN)]

    q = x * NZ + z
    for d in range(1, NY):
        arrived(yrc.at[yd(-d)], ysem, (d,))
    for s in range(G):
        p = pos[s]
        v = yrc[lax.div(p, jnp.int32(CAP)), lax.rem(p, jnp.int32(CAP))]
        alive = r * G + s < bcnt[k]
        gath[q, s] = jnp.where(alive, v.astype(F32), 0.0).astype(BF)

    up, down = dev_z(1), dev_z(-1)
    mid = NZ // 2

    def forward(e, h, piece):
        if h < mid or (h == mid and e < NX // 2):
            send(gath.at[piece], gath.at[piece], agu, (e, h), up)
        if h < mid or (h == mid and e >= NX // 2):
            send(gath.at[piece], gath.at[piece], agd, (e, h), down)

    forward(0, 1, q)
    for d in range(1, NX):
        send(gath.at[q], gath.at[q], agx, (d,), dev_x(d))
    for e in range(1, NX):
        piece = xd(-e) * NZ + z
        arrived(gath.at[piece], agx, (e,))
        forward(e, 1, piece)
    for h in range(1, mid + 1):
        for e in range(NX):
            if h < mid or (h == mid and e < NX // 2):
                piece = xd(-e) * NZ + zd(-h)
                arrived(gath.at[piece], agu, (e, h))
                if h + 1 < mid or (h + 1 == mid and e < NX // 2):
                    send(gath.at[piece], gath.at[piece], agu, (e, h + 1), up)
            if h < mid or (h == mid and e >= NX // 2):
                piece = xd(-e) * NZ + zd(h)
                arrived(gath.at[piece], agd, (e, h))
                if h + 1 < mid or (h + 1 == mid and e >= NX // 2):
                    send(gath.at[piece], gath.at[piece], agd, (e, h + 1), down)

    loads[3].wait()
    for s in range(G):
        lhs[:, s * BLOCK:(s + 1) * BLOCK] = gath[:, s].reshape(sz.C, BLOCK)
    prod = jnp.dot(lhs[...], coup_v[...], preferred_element_type=F32)
    ycs[...] = prod.reshape(NY, sz.CY, sz.S3)
    for d in far_first(NY):
        y1s[d] = ycs[yd(d)].astype(BF)
        send(y1s.at[d], ycr.at[d], y1sem, (d,), dev_y(d))

    for d in range(1, NZ):
        arrived(o1.at[zd(-d)], o1sem, (d,))
    for d in range(1, NX):
        send(o1, o2.at[x], o2sem, (d,), dev_x(d))
    o2[x] = o1[...]

    acc = ycs[r]
    for d in range(1, NY):
        arrived(ycr.at[d], y1sem, (d,))
        acc = acc + ycr[d].astype(F32)
    mine_y = pl.ds(pl.multiple_of(r * sz.CY, sz.CY), sz.CY)
    red[r] = (crhs_t[mine_y, :] - acc).astype(BF)
    for d in far_first(NY):
        send(red.at[r], red.at[r], y2sem, (d,), dev_y(d))

    for d in range(1, NX):
        arrived(o2.at[xd(-d)], o2sem, (d,))
    for b in range(sz.SPAN):
        ot[b * BLOCK:(b + 1) * BLOCK, :] = o2[:, :, b].astype(F32).reshape(sz.C, BLOCK).T
    first_row = sz.TZ * z + (2 * x + k) * sz.TO - first_block(z) * BLOCK
    rout[...] = ot[pl.ds(pl.multiple_of(first_row, 8), sz.TO), :].astype(BF)

    for d in range(1, NY):
        arrived(red.at[yd(-d)], y2sem, (d,))
    reduced = red[...].reshape(sz.C, sz.S3)
    rows_z = NX * sz.TC
    for d in far_first(NZ) + [0]:
        rows = pl.ds(pl.multiple_of(zd(d) * rows_z, rows_z), rows_z)
        v = lax.dot_general(cit[rows, :], reduced, (((1,), (1,)), ((), ())), preferred_element_type=F32)
        p5f[d] = v.reshape(NX, sz.TC, sz.C)
        for e in range(1, NX):
            p5s[d, e] = p5f[d, xd(e)].astype(BF)
            send(p5s.at[d, e], p5r.at[d, e], p5sem, (d, e), dev_x(e))
    for d in far_first(NZ) + [0]:
        acc = p5f[d, x]
        for e in range(1, NX):
            arrived(p5r.at[d, e], p5sem, (d, e))
            acc = acc + p5r[d, e].astype(F32)
        if d:
            z5s[d] = acc.astype(BF)
            send(z5s.at[d], z5r.at[d], z5sem, (d,), dev_z(d))
    for d in far_first(NZ):
        arrived(z5r.at[d], z5sem, (d,))
        acc = acc + z5r[d].astype(F32)
    cout[0] = acc.astype(BF)

    for cp in sent:
        cp.wait_send()


def per_device(mesh, root_rhs, root_inverse, child_rhs, child_inverse, coupling, block_map, block_count):
    sz = Sizes(mesh, root_rhs, root_inverse, child_inverse, coupling, block_map)
    NX, NZ, NY, NCH, CB, Q, G = sz.NX, sz.NZ, sz.NY, sz.NCH, sz.CB, sz.Q, sz.G
    vmem = pl.BlockSpec(memory_space=pltpu.VMEM)
    smem = pl.BlockSpec(memory_space=pltpu.SMEM)
    hbm = pl.BlockSpec(memory_space=pl.ANY)

    def dma(*shape):
        return pltpu.SemaphoreType.DMA((2,) + shape)

    scratch = dict(
        rinv_v=pltpu.VMEM((sz.S1, sz.T1), BF),
        coup_v=pltpu.VMEM((sz.U, sz.S3), BF),
        cinv_v=pltpu.VMEM((sz.S3, sz.T3), BF),
        cit=pltpu.VMEM((sz.T3, sz.S3), BF),
        rhs_t=pltpu.VMEM((sz.C, sz.S1), BF),
        crhs_t=pltpu.VMEM((sz.C, sz.S3), F32),
        cs=pltpu.VMEM((NCH, Q, CB, 8, BLOCK), F32),
        cr=pltpu.VMEM((NCH, Q, CB, 8, BLOCK), F32),
        own=pltpu.VMEM((NCH, Q, CB, 8, BLOCK), F32),
        xs=pltpu.VMEM((NCH, NX, NZ, CB, 8, BLOCK), BF),
        xr=pltpu.VMEM((NCH, NX, NZ, CB, 8, BLOCK), BF),
        zacc=pltpu.VMEM((NCH, NZ, CB, 8, BLOCK), F32),
        zs=pltpu.VMEM((NCH, NZ, CB, 8, BLOCK), BF),
        zr=pltpu.VMEM((NCH, NZ, CB, 8, BLOCK), BF),
        sol=pltpu.VMEM((sz.NB, 8, BLOCK), BF),
        ysd=pltpu.VMEM((NY, CAP, 8, BLOCK), BF),
        yrc=pltpu.VMEM((NY, CAP, 8, BLOCK), BF),
        gath=pltpu.VMEM((Q, G, 8, BLOCK), BF),
        lhs=pltpu.VMEM((sz.C, sz.U), BF),
        ycs=pltpu.VMEM((NY, sz.CY, sz.S3), F32),
        y1s=pltpu.VMEM((NY, sz.CY, sz.S3), BF),
        ycr=pltpu.VMEM((NY, sz.CY, sz.S3), BF),
        red=pltpu.VMEM((NY, sz.CY, sz.S3), BF),
        o1=pltpu.VMEM((NZ, sz.SPAN, 8, BLOCK), BF),
        o2=pltpu.VMEM((NX, NZ, sz.SPAN, 8, BLOCK), BF),
        ot=pltpu.VMEM((sz.SPAN * BLOCK, sz.C), F32),
        p5f=pltpu.VMEM((NZ, NX, sz.TC, sz.C), F32),
        p5s=pltpu.VMEM((NZ, NX, sz.TC, sz.C), BF),
        p5r=pltpu.VMEM((NZ, NX, sz.TC, sz.C), BF),
        z5s=pltpu.VMEM((NZ, sz.TC, sz.C), BF),
        z5r=pltpu.VMEM((NZ, sz.TC, sz.C), BF),
        sel=pltpu.SMEM((NY * CAP,), jnp.int32),
        pos=pltpu.SMEM((G,), jnp.int32),
        lsem=pltpu.SemaphoreType.DMA((4,)),
        csem=dma(NCH),
        xsem=dma(NCH, NX),
        zsem=dma(NCH, NZ),
        c2sem=dma(1),
        ysem=dma(NY),
        o1sem=dma(NZ),
        o2sem=dma(NX),
        agx=dma(NX),
        agu=dma(NX, NZ // 2 + 1),
        agd=dma(NX, NZ // 2 + 1),
        y1sem=dma(NY),
        y2sem=dma(NY),
        p5sem=dma(NZ, NX),
        z5sem=dma(NZ),
    )
    names = list(scratch)

    def body(*refs):
        kernel(sz, *refs[:9], **dict(zip(names, refs[9:])))

    return pl.pallas_call(
        body,
        name="backward",
        out_shape=(
            jax.ShapeDtypeStruct((sz.TO, sz.C), BF),
            jax.ShapeDtypeStruct((1, sz.TC, sz.C), BF),
        ),
        in_specs=[vmem, hbm, vmem, hbm, hbm, smem, smem],
        out_specs=(vmem, vmem),
        scratch_shapes=list(scratch.values()),
        compiler_params=pltpu.CompilerParams(
            collective_id=0, has_side_effects=True, vmem_limit_bytes=56 * 1024 * 1024
        ),
    )(root_rhs, root_inverse, child_rhs, child_inverse, coupling, block_map, block_count)


def solution(mesh):
    in_specs = (
        P(("col", "cores"), None),
        P(("col", "cores"), "row"),
        P("cores", "col", None),
        P("cores", "col", "row"),
        P("cores", "row", "col"),
        P(),
        P(),
    )
    out_specs = (P(("row", "col", "cores"), None), P("cores", ("row", "col"), None))
    return jax.shard_map(
        functools.partial(per_device, mesh),
        mesh=mesh, in_specs=in_specs, out_specs=out_specs, check_vma=False,
    )
```

time: 616 us -> 91 us (0.15)
  the two profiles are of different devices: /device:TPU:40 before, /device:TPU:8 now
where the time goes in v1:
time: 91 us; the launch traced here: 90.6 us
  Pallas kernels  83.5 us (92%)
  local copies, waits for them, and re-layouts  6.5 us (7%)
    pallas_call x1, Pallas kernels, per_device(): pl.pallas_call(body, name='backward', out_shape=(jax.ShapeDtypeStruct((sz...  83.5 us
    unnamed x3, local copies, waits for them, and re-layouts  6.5 us

profile of v1, /device:TPU:8, one launch (start us, length us, event | category | flops | bytes accessed | tf_op | source)
XLA Modules:
  0.0 90.6 jit_solution(10758150848396559536)
XLA Ops:
  0.6 3.8 %copy.9.refs_4_ = bf16[1,2560,320]{2,1,0:T(8,128)(2,1)} copy(bf16[1,2560,320]{1,2,0:T(8,128)(2,1)} %param.11) | data formatting | bytes 3276800 | tf_op args[4]
  4.5 83.5 %backward.1 = (bf16[40,256]{1,0:T(8,128)(2,1)}, bf16[1,40,256]{2,1,0:T(8,128)(2,1)}) custom-call(bf16[320,256]{1,0:T(8,128)(2,1)} %refs_0_.1, bf16[320,2560]{1,0:T(8,128)(2,1)} %refs_1_.1, bf16[1,320,256]{2,1,0:T(8,128)(2,1)} %refs_2_.1, bf16[1,320,1280]{2,1,0:T(8,128)(2,1)} %refs_3_.1, bf16[1,2560,320]{2,1,0:T(8,128)(2,1)} %copy.9.refs_4_, ...), custom_call_target="tpu_custom_call" | custom-call | tf_op jit(solution)/shard_map/backward/pallas_call | solution.py:365
  88.0 1.3 %copy.12 = bf16[40,256]{1,0:T(8,128)(2,1)} copy(bf16[40,256]{1,0:T(8,128)(2,1)} %get-tuple-element.4) | data formatting | bytes 40960
  89.3 1.3 %copy.13 = bf16[1,40,256]{2,1,0:T(8,128)(2,1)} copy(bf16[1,40,256]{2,1,0:T(8,128)(2,1)} %get-tuple-element.5) | data formatting | bytes 40960

commit v2 on v1

v2 whole, which is shorter than its diff:
```python
import functools

import jax
import jax.numpy as jnp
from jax import lax
from jax.experimental import pallas as pl
from jax.experimental.pallas import tpu as pltpu
from jax.sharding import PartitionSpec as P

BLOCK = 128
CAP = 3
GRID = {32: (4, 8), 4: (2, 2)}
MESH = pl.DeviceIdType.MESH
BF = jnp.bfloat16
F32 = jnp.float32


class Sizes:
    def __init__(self, mesh, root_rhs, root_inverse, child_inverse, coupling):
        self.NY = mesh.shape["row"]
        self.NX, self.NZ = GRID[mesh.shape["col"]]
        self.Q = self.NX * self.NZ
        self.S1, self.C = root_rhs.shape
        self.T1 = root_inverse.shape[1]
        self.NB = self.T1 // BLOCK
        self.HB = self.NB // 2
        self.S3, self.T3 = child_inverse.shape[1:]
        self.U = coupling.shape[1]
        self.G = self.U // BLOCK
        self.HA = max(self.G // 5, 1)
        self.CY = self.C // self.NY
        self.TO = self.T1 // (2 * self.Q)
        self.TC = self.T3 // self.Q
        self.TZ = self.T1 // self.NZ
        self.AB = max(8 * self.HB // 10, 1)
        self.RA = self.TC - 8
        starts = [self.TZ * z // BLOCK for z in range(self.NZ)]
        ends = [-(-self.TZ * (z + 1) // BLOCK) for z in range(self.NZ)]
        self.SPAN = max(e - s for s, e in zip(starts, ends))
        self.full = self.S3 // BLOCK
        self.packed = (self.CY * self.S3 // BLOCK, BLOCK)

    def pack(self, v):
        h = self.CY // 2
        parts = [v[:, i * BLOCK:(i + 1) * BLOCK] for i in range(self.full)]
        if self.S3 % BLOCK:
            rest = v[:, self.full * BLOCK:]
            parts.append(jnp.concatenate([rest[:h], rest[h:]], axis=1))
        return jnp.concatenate(parts, axis=0)

    def unpack(self, v):
        h, n = self.CY // 2, self.CY
        parts = [v[i * n:(i + 1) * n] for i in range(self.full)]
        if self.S3 % BLOCK:
            rest = v[self.full * n:]
            parts.append(jnp.concatenate([rest[:, :BLOCK // 2], rest[:, BLOCK // 2:]], axis=0))
        return jnp.concatenate(parts, axis=1)


def far_first(n):
    return sorted(range(1, n), key=lambda d: (-min(d, n - d), d))


def kernel(
    sz, rrhs, rinv, crhs, cinv, coup, bmap, bcnt, out, *,
    rrhs_v, rinv_v, crhs_v, coup_v, cinv_v, bmap_s, bcnt_s, cit, rhs_t, crhs_t, cs, cr, own, xs, xr, zs, zr, ws, wr, ts, tr, sol,
    ysd, yrc, ga, gb, lhs, ycs, y1s, ycr, red, red_s, o1, o2, ot, p5f, p5s, p5r, z5s, z5r, w5s, w5r, t5s, t5r, sel, pos,
    lsem, csem, xsem, zsem, wsem, tsem, c2sem, ysem, o1sem, o2sem, agx, aga, agz, agc, y1sem, y2sem, p5sem, z5sem, w5sem, t5sem,
):
    NX, NZ, NY, HB, NB, G, HA = sz.NX, sz.NZ, sz.NY, sz.HB, sz.NB, sz.G, sz.HA
    r, c, k = lax.axis_index("row"), lax.axis_index("col"), lax.axis_index("cores")
    z, x = c // NX, lax.rem(c, NX)
    AB, RA = sz.AB, sz.RA

    def xd(d):
        return lax.rem(x + d + NX, NX)

    def zd(d):
        return lax.rem(z + d + NZ, NZ)

    def yd(d):
        return lax.rem(r + d + NY, NY)

    def dev_x(d):
        return (r, z * NX + xd(d), k)

    def dev_z(d):
        return (r, zd(d) * NX + x, k)

    def dev_y(d):
        return (yd(d), c, k)

    def near(i):
        if isinstance(i, int):
            return NZ - (i + 1) // 2 if i % 2 else i // 2
        return jnp.where(lax.rem(i, 2) == 1, NZ - (i + 1) // 2, i // 2)

    dev_c = (r, c, 1 - k)
    sent = []

    def send(src, dst, sem, idx, dev, to=None):
        cp = pltpu.make_async_remote_copy(
            src_ref=src, dst_ref=dst, send_sem=sem.at[(0,) + idx], recv_sem=sem.at[(1,) + (to or idx)],
            device_id=dev, device_id_type=MESH,
        )
        cp.start()
        sent.append(cp)

    def drain():
        for cp in sent:
            cp.wait_send()
        sent.clear()

    def arrived(ref, sem, idx):
        pltpu.make_async_remote_copy(
            src_ref=ref, dst_ref=ref, send_sem=sem.at[(0,) + idx], recv_sem=sem.at[(1,) + idx],
            device_id=dev_c, device_id_type=MESH,
        ).wait_recv()

    half = HB * BLOCK
    theirs = pl.ds(pl.multiple_of((1 - k) * half, BLOCK), half)
    ours = pl.ds(pl.multiple_of(k * half, BLOCK), half)
    pairs = [
        (rrhs, rrhs_v), (rinv.at[:, theirs], rinv_v.at[:, theirs]), (rinv.at[:, ours], rinv_v.at[:, ours]),
        (bmap, bmap_s), (bcnt, bcnt_s), (cinv.at[0], cinv_v), (crhs.at[0], crhs_v), (coup.at[0], coup_v),
    ]
    loads = [pltpu.make_async_copy(a, b, lsem.at[i]) for i, (a, b) in enumerate(pairs)]
    for cp in loads:
        cp.start()
    load_rrhs, load_theirs, load_ours, load_map, load_count, load_cinv, load_crhs, load_coup = loads

    barrier = pltpu.get_barrier_semaphore()
    peers = (
        [dev_c]
        + [dev_x(d) for d in range(1, NX)]
        + [dev_z(d) for d in range(1, NZ)]
        + [dev_y(d) for d in range(1, NY)]
    )
    for dev in peers:
        pl.semaphore_signal(barrier, inc=1, device_id=dev, device_id_type=MESH)

    def partial(which, dst):
        for b in range(0, HB, 2):
            off = pl.multiple_of(which * half + b * BLOCK, BLOCK)
            v = jnp.dot(rhs_t[...], rinv_v[:, pl.ds(off, 2 * BLOCK)], preferred_element_type=F32)
            for i in range(2):
                dst[:, :, b + i] = v[:, i * BLOCK:(i + 1) * BLOCK].reshape(NZ, NX, 8, BLOCK)

    order = far_first(NZ) + [0]
    load_rrhs.wait()
    rhs_t[...] = rrhs_v[...].astype(F32).T.astype(BF)
    load_theirs.wait()
    partial(1 - k, cs)
    load_ours.wait()
    partial(k, own)
    pl.semaphore_wait(barrier, len(peers))
    for d in order:
        send(cs.at[zd(d)], cr.at[zd(d)], csem, (d,), dev_c)

    for d in order:
        arrived(cr.at[zd(d)], csem, (d,))
        if d:
            ws[d] = (own[zd(d), :, AB:] + cr[zd(d), :, AB:]).astype(BF)
            send(ws.at[d], wr.at[d], wsem, (d,), dev_z(d), to=(0,))
        for e in range(1, NX):
            xs[d, e] = (own[zd(d), xd(e), :AB] + cr[zd(d), xd(e), :AB]).astype(BF)
            send(xs.at[d, e], xr.at[d, e], xsem, (d, e), dev_x(e), to=(d, 0))
    for d in order:
        acc = own[zd(d), x, :AB] + cr[zd(d), x, :AB]
        arrived(xr.at[d, pl.ds(1, NX - 1)], xsem, (d, 0))
        for e in range(1, NX):
            acc = acc + xr[d, e].astype(F32)
        if d:
            zs[d] = acc.astype(BF)
            send(zs.at[d], zr.at[d], zsem, (d,), dev_z(d))
        else:
            own[z, x, :AB] = acc
    acc = own[z, :, AB:] + cr[z, :, AB:]
    arrived(wr.at[pl.ds(1, NZ - 1)], wsem, (0,))
    for d in range(1, NZ):
        acc = acc + wr[d].astype(F32)
    own[z, :, AB:] = acc
    for e in range(1, NX):
        ts[e] = own[z, xd(e), AB:].astype(BF)
        send(ts.at[e], tr.at[e], tsem, (e,), dev_x(e), to=(0,))

    def choose(t, _):
        cnt = jnp.int32(0)
        got = [jnp.int32(0)] * CAP
        for s in range(G):
            b = bmap_s[k, t * G + s] - r * NB
            inside = jnp.logical_and(b >= 0, b < NB)
            for j in range(CAP):
                got[j] = jnp.where(jnp.logical_and(inside, cnt == j), b, got[j])
            cnt = cnt + jnp.where(inside, 1, 0)
        for j in range(CAP):
            sel[t * CAP + j] = got[j]
        return 0

    load_map.wait()
    load_count.wait()
    lax.fori_loop(0, NY, choose, 0)

    acc = own[z, x, :AB]
    for d in far_first(NZ):
        arrived(zr.at[d], zsem, (d,))
        acc = acc + zr[d].astype(F32)
    sol[pl.ds(k * HB, AB)] = acc.astype(BF)
    acc = own[z, x, AB:]
    arrived(tr.at[pl.ds(1, NX - 1)], tsem, (0,))
    for e in range(1, NX):
        acc = acc + tr[e].astype(F32)
    sol[pl.ds(k * HB + AB, HB - AB)] = acc.astype(BF)
    mine = pl.ds(k * HB, HB)
    send(sol.at[mine], sol.at[mine], c2sem, (0,), dev_c)
    arrived(sol.at[pl.ds((1 - k) * HB, HB)], c2sem, (0,))

    for d in far_first(NY) + [0]:
        t = yd(d)
        for j in range(CAP):
            v = sol[sel[t * CAP + j]]
            if d:
                ysd[d, j] = v
            else:
                yrc[r * CAP + j] = v
        if d:
            send(ysd.at[d], yrc.at[pl.ds(r * CAP, CAP)], ysem, (d,), dev_y(d))

    ranges = [lax.div(bmap_s[k, r * G + s], jnp.int32(NB)) for s in range(G)]
    for s in range(G):
        rank = jnp.int32(0)
        for e in range(s):
            rank = rank + jnp.where(ranges[e] == ranges[s], 1, 0)
        pos[s] = ranges[s] * CAP + jnp.minimum(rank, CAP - 1)
    drain()
    for d in range(1, NY):
        arrived(yrc.at[pl.ds(yd(-d) * CAP, CAP)], ysem, (d,))
    for s in [*range(HA, G), *range(HA)]:
        v = yrc[pos[s]]
        alive = r * G + s < bcnt_s[k]
        v = jnp.where(alive, v.astype(F32), 0.0).astype(BF)
        if s < HA:
            ga[0, 0, s] = v
        else:
            gb[0, 0, s - HA] = v

    for e in range(1, NX):
        send(ga.at[0, 0], ga.at[0, e], agx, (e,), dev_x(e))
    for i in range(1, NZ):
        send(gb.at[0, 0], gb.at[0, i], agz, (i,), dev_z(near(i)))

    def spread(i):
        for e in range(1, NX):
            send(gb.at[0, i], gb.at[e, i], agc, (e, i), dev_x(e), to=(e, 0))

    spread(0)
    for e in range(1, NX):
        arrived(ga.at[0, e], agx, (e,))
    for i in range(1, NZ):
        send(ga.at[0], ga.at[i], aga, (i,), dev_z(near(i)))
    for i in range(1, NZ):
        arrived(gb.at[0, i], agz, (i,))
        spread(i)
    load_coup.wait()

    for i in range(1, NZ):
        arrived(ga.at[i], aga, (i,))
    for s in range(HA):
        lhs[:, s * BLOCK:(s + 1) * BLOCK] = ga[:, :, s].reshape(sz.C, BLOCK)
    for e in range(1, NX):
        arrived(gb.at[e], agc, (e, 0))
    for s in range(HA, G):
        v = jnp.stack([gb[e, :, s - HA] for e in range(NX)], axis=1)
        lhs[:, s * BLOCK:(s + 1) * BLOCK] = v.reshape(sz.C, BLOCK)
    prod = lax.dot_general(lhs[...], coup_v[...], (((1,), (1,)), ((), ())), preferred_element_type=F32)
    for t in range(NY):
        ycs[t] = sz.pack(prod[t * sz.CY:(t + 1) * sz.CY, :])
    for d in far_first(NY):
        y1s[d] = ycs[yd(d)].astype(BF)
        send(y1s.at[d], ycr.at[d], y1sem, (d,), dev_y(d))

    def first_block(zz):
        return (sz.TZ * zz) // BLOCK

    for d in far_first(NZ):
        send(sol.at[pl.ds(first_block(zd(d)), sz.SPAN)], o1.at[z], o1sem, (d,), dev_z(d))
    o1[z] = sol[pl.ds(first_block(z), sz.SPAN)]

    load_crhs.wait()
    crhs_t[...] = crhs_v[...].astype(F32).T
    load_cinv.wait()
    for j in range(sz.T3 // BLOCK):
        cols = slice(j * BLOCK, (j + 1) * BLOCK)
        cit[cols, :] = cinv_v[:, cols].astype(F32).T.astype(BF)

    acc = ycs[r]
    for d in far_first(NY)[::-1]:
        arrived(ycr.at[d], y1sem, (d,))
        acc = acc + ycr[d].astype(F32)
    acc = sz.unpack(acc)
    from_z = zd(-near(r))
    diff = []
    for e in range(NX):
        rows = pl.ds(pl.multiple_of((from_z * NX + xd(-e)) * 8, 8), 8)
        diff.append(crhs_t[rows, :] - acc[e * 8:(e + 1) * 8, :])
    red[0] = sz.pack(jnp.concatenate(diff, axis=0)).astype(BF)
    for d in far_first(NY):
        send(red.at[0], red.at[d], y2sem, (d,), dev_y(d))

    for d in range(1, NZ):
        arrived(o1.at[zd(-d)], o1sem, (d,))
    for d in range(1, NX):
        send(o1, o2.at[x], o2sem, (d,), dev_x(d))
    o2[x] = o1[...]
    drain()
    for d in range(1, NX):
        arrived(o2.at[xd(-d)], o2sem, (d,))
    for b in range(sz.SPAN):
        v = jnp.stack([o2[e, :, b] for e in range(NX)], axis=1)
        ot[b * BLOCK:(b + 1) * BLOCK, :] = v.astype(F32).reshape(sz.C, BLOCK).T
    first_row = sz.TZ * z + (2 * x + k) * sz.TO - first_block(z) * BLOCK
    out[:sz.TO] = ot[pl.ds(pl.multiple_of(first_row, 8), sz.TO), :].astype(BF)

    for d in range(1, NY):
        arrived(red.at[d], y2sem, (d,))
    for d in range(NY):
        v = sz.unpack(red[d].astype(F32)).astype(BF).reshape(NX, 8, sz.S3)
        for e in range(NX):
            red_s[zd(-near(yd(-d))), xd(-e)] = v[e]
    reduced = red_s[...].reshape(sz.C, sz.S3)
    rows_z = NX * sz.TC
    for d in order:
        rows = pl.ds(pl.multiple_of(zd(d) * rows_z, rows_z), rows_z)
        v = lax.dot_general(cit[rows, :], reduced, (((1,), (1,)), ((), ())), preferred_element_type=F32)
        p5f[d] = v.reshape(NX, sz.TC, sz.C)
        if d:
            w5s[d] = p5f[d, :, RA:].astype(BF)
            send(w5s.at[d], w5r.at[d], w5sem, (d,), dev_z(d), to=(0,))
        for e in range(1, NX):
            p5s[d, e] = p5f[d, xd(e), :RA].astype(BF)
            send(p5s.at[d, e], p5r.at[d, e], p5sem, (d, e), dev_x(e), to=(d, 0))
    for d in order:
        acc = p5f[d, x, :RA]
        arrived(p5r.at[d, pl.ds(1, NX - 1)], p5sem, (d, 0))
        for e in range(1, NX):
            acc = acc + p5r[d, e].astype(F32)
        if d:
            z5s[d] = acc.astype(BF)
            send(z5s.at[d], z5r.at[d], z5sem, (d,), dev_z(d))
    p5f[0, x, :RA] = acc
    acc = p5f[0, :, RA:]
    arrived(w5r.at[pl.ds(1, NZ - 1)], w5sem, (0,))
    for d in range(1, NZ):
        acc = acc + w5r[d].astype(F32)
    p5f[0, :, RA:] = acc
    for e in range(1, NX):
        t5s[e] = p5f[0, xd(e), RA:].astype(BF)
        send(t5s.at[e], t5r.at[e], t5sem, (e,), dev_x(e), to=(0,))
    drain()
    acc = p5f[0, x, :RA]
    for d in far_first(NZ):
        arrived(z5r.at[d], z5sem, (d,))
        acc = acc + z5r[d].astype(F32)
    out[sz.TO:sz.TO + RA] = acc.astype(BF)
    acc = p5f[0, x, RA:]
    arrived(t5r.at[pl.ds(1, NX - 1)], t5sem, (0,))
    for e in range(1, NX):
        acc = acc + t5r[e].astype(F32)
    out[sz.TO + RA:] = acc.astype(BF)


def per_device(mesh, root_rhs, root_inverse, child_rhs, child_inverse, coupling, block_map, block_count):
    sz = Sizes(mesh, root_rhs, root_inverse, child_inverse, coupling)
    coupling = jnp.swapaxes(coupling, 1, 2)
    NX, NZ, NY, HB, Q, G, HA = sz.NX, sz.NZ, sz.NY, sz.HB, sz.Q, sz.G, sz.HA
    AB, RA = sz.AB, sz.RA
    vmem = pl.BlockSpec(memory_space=pltpu.VMEM)
    hbm = pl.BlockSpec(memory_space=pl.ANY)

    def dma(*shape):
        return pltpu.SemaphoreType.DMA((2,) + shape)

    scratch = dict(
        rrhs_v=pltpu.VMEM((sz.S1, sz.C), BF),
        rinv_v=pltpu.VMEM((sz.S1, sz.T1), BF),
        crhs_v=pltpu.VMEM((sz.S3, sz.C), BF),
        coup_v=pltpu.VMEM((sz.S3, sz.U), BF),
        cinv_v=pltpu.VMEM((sz.S3, sz.T3), BF),
        bmap_s=pltpu.SMEM(block_map.shape, jnp.int32),
        bcnt_s=pltpu.SMEM(block_count.shape, jnp.int32),
        cit=pltpu.VMEM((sz.T3, sz.S3), BF),
        rhs_t=pltpu.VMEM((sz.C, sz.S1), BF),
        crhs_t=pltpu.VMEM((sz.C, sz.S3), F32),
        cs=pltpu.VMEM((NZ, NX, HB, 8, BLOCK), F32),
        cr=pltpu.VMEM((NZ, NX, HB, 8, BLOCK), F32),
        own=pltpu.VMEM((NZ, NX, HB, 8, BLOCK), F32),
        xs=pltpu.VMEM((NZ, NX, AB, 8, BLOCK), BF),
        xr=pltpu.VMEM((NZ, NX, AB, 8, BLOCK), BF),
        zs=pltpu.VMEM((NZ, AB, 8, BLOCK), BF),
        zr=pltpu.VMEM((NZ, AB, 8, BLOCK), BF),
        ws=pltpu.VMEM((NZ, NX, HB - AB, 8, BLOCK), BF),
        wr=pltpu.VMEM((NZ, NX, HB - AB, 8, BLOCK), BF),
        ts=pltpu.VMEM((NX, HB - AB, 8, BLOCK), BF),
        tr=pltpu.VMEM((NX, HB - AB, 8, BLOCK), BF),
        sol=pltpu.VMEM((sz.NB, 8, BLOCK), BF),
        ysd=pltpu.VMEM((NY, CAP, 8, BLOCK), BF),
        yrc=pltpu.VMEM((NY * CAP, 8, BLOCK), BF),
        ga=pltpu.VMEM((NZ, NX, HA, 8, BLOCK), BF),
        gb=pltpu.VMEM((NX, NZ, G - HA, 8, BLOCK), BF),
        lhs=pltpu.VMEM((sz.C, sz.U), BF),
        ycs=pltpu.VMEM((NY,) + sz.packed, F32),
        y1s=pltpu.VMEM((NY,) + sz.packed, BF),
        ycr=pltpu.VMEM((NY,) + sz.packed, BF),
        red=pltpu.VMEM((NY,) + sz.packed, BF),
        red_s=pltpu.VMEM((NZ, NX, 8, sz.S3), BF),
        o1=pltpu.VMEM((NZ, sz.SPAN, 8, BLOCK), BF),
        o2=pltpu.VMEM((NX, NZ, sz.SPAN, 8, BLOCK), BF),
        ot=pltpu.VMEM((sz.SPAN * BLOCK, sz.C), F32),
        p5f=pltpu.VMEM((NZ, NX, sz.TC, sz.C), F32),
        p5s=pltpu.VMEM((NZ, NX, RA, sz.C), BF),
        p5r=pltpu.VMEM((NZ, NX, RA, sz.C), BF),
        z5s=pltpu.VMEM((NZ, RA, sz.C), BF),
        z5r=pltpu.VMEM((NZ, RA, sz.C), BF),
        w5s=pltpu.VMEM((NZ, NX, sz.TC - RA, sz.C), BF),
        w5r=pltpu.VMEM((NZ, NX, sz.TC - RA, sz.C), BF),
        t5s=pltpu.VMEM((NX, sz.TC - RA, sz.C), BF),
        t5r=pltpu.VMEM((NX, sz.TC - RA, sz.C), BF),
        sel=pltpu.SMEM((NY * CAP,), jnp.int32),
        pos=pltpu.SMEM((G,), jnp.int32),
        lsem=pltpu.SemaphoreType.DMA((8,)),
        csem=dma(NZ),
        xsem=dma(NZ, NX),
        zsem=dma(NZ),
        wsem=dma(NZ),
        tsem=dma(NX),
        c2sem=dma(1),
        ysem=dma(NY),
        o1sem=dma(NZ),
        o2sem=dma(NX),
        agx=dma(NX),
        aga=dma(NZ),
        agz=dma(NZ),
        agc=dma(NX, NZ),
        y1sem=dma(NY),
        y2sem=dma(NY),
        p5sem=dma(NZ, NX),
        z5sem=dma(NZ),
        w5sem=dma(NZ),
        t5sem=dma(NX),
    )
    names = list(scratch)

    def body(*refs):
        kernel(sz, *refs[:8], **dict(zip(names, refs[8:])))

    both = pl.pallas_call(
        body,
        name="backward",
        out_shape=jax.ShapeDtypeStruct((sz.TO + sz.TC, sz.C), BF),
        in_specs=[hbm] * 7,
        out_specs=vmem,
        scratch_shapes=list(scratch.values()),
        compiler_params=pltpu.CompilerParams(
            collective_id=0, has_side_effects=True, vmem_limit_bytes=56 * 1024 * 1024
        ),
    )(root_rhs, root_inverse, child_rhs, child_inverse, coupling, block_map, block_count)
    return both[:sz.TO], both[sz.TO:][None]


def solution(mesh):
    in_specs = (
        P(("col", "cores"), None),
        P(("col", "cores"), "row"),
        P("cores", "col", None),
        P("cores", "col", "row"),
        P("cores", "row", "col"),
        P(),
        P(),
    )
    out_specs = (P(("row", "col", "cores"), None), P("cores", ("row", "col"), None))
    return jax.shard_map(
        functools.partial(per_device, mesh),
        mesh=mesh, in_specs=in_specs, out_specs=out_specs, check_vma=False,
    )
```

time: 91 us -> 76.3 us (0.84)
  Pallas kernels: 83.5 us -> 74.2 us
  local copies, waits for them, and re-layouts: 6.5 us -> 1.36 us
    pallas_call x1, Pallas kernels: 83.5 us -> 74.2 us  [per_device(): pl.pallas_call(body, name='backward', out_shape=jax.ShapeDtypeStruct((sz....]
    unnamed x3 -> x0, local copies, waits for them, and re-layouts: 6.5 us -> none
    broadcast_in_dim x0 -> x1, local copies, waits for them, and re-layouts: none -> 1.36 us  [per_device(): return (both[:sz.TO], both[sz.TO:][None])]
where the time goes in v2:
time: 76.3 us; the launch traced here: 76.2 us
  Pallas kernels  74.2 us (97%)
  local copies, waits for them, and re-layouts  1.36 us (2%)
    pallas_call x1, Pallas kernels, per_device(): pl.pallas_call(body, name='backward', out_shape=jax.ShapeDtypeStruct((sz....  74.2 us

profile of v2, /device:TPU:8, one launch (start us, length us, event | category | flops | bytes accessed | tf_op | source)
XLA Modules:
  0.0 76.2 jit_solution(12844551079845968418)
XLA Ops:
  0.6 74.2 %backward.1 = bf16[80,256]{1,0:T(8,128)(2,1)} custom-call(bf16[320,256]{1,0:T(8,128)(2,1)} %refs_0_.1, bf16[320,2560]{1,0:T(8,128)(2,1)} %refs_1_.1, bf16[1,320,256]{2,1,0:T(8,128)(2,1)} %refs_2_.1, bf16[1,320,1280]{2,1,0:T(8,128)(2,1)} %refs_3_.1, bf16[1,320,2560]{2,1,0:T(8,128)(2,1)} %bitcast.3, s32[2,160]{1,0:T(2,128)} %refs_5_.1, s32[2]{0:T(128)} %refs_6_.1), custom_call_target="tpu_custom_call" | custom-call | tf_op jit(solution)/shard_map/backward/pallas_call | solution.py:456
  74.8 1.4 %slice_bitcast_fusion = (bf16[1,40,256]{2,1,0:T(8,128)(2,1)}, bf16[40,256]{1,0:T(8,128)(2,1)}) fusion(bf16[80,256]{1,0:T(8,128)(2,1)} %backward.1), kind=kLoop, calls=%fused_computation | loop fusion | bytes 81920 | tf_op jit(solution)/shard_map/broadcast_in_dim | solution.py:467

commit v3 on v2

--- a/solution.py
+++ b/solution.py
@@ -125,7 +125,7 @@
         (bmap, bmap_s), (bcnt, bcnt_s), (cinv.at[0], cinv_v), (crhs.at[0], crhs_v), (coup.at[0], coup_v),
     ]
     loads = [pltpu.make_async_copy(a, b, lsem.at[i]) for i, (a, b) in enumerate(pairs)]
-    for cp in loads:
+    for cp in loads[:3]:
         cp.start()
     load_rrhs, load_theirs, load_ours, load_map, load_count, load_cinv, load_crhs, load_coup = loads
 
@@ -153,6 +153,8 @@
     partial(1 - k, cs)
     load_ours.wait()
     partial(k, own)
+    for cp in loads[3:]:
+        cp.start()
     pl.semaphore_wait(barrier, len(peers))
     for d in order:
         send(cs.at[zd(d)], cr.at[zd(d)], csem, (d,), dev_c)
@@ -162,7 +164,7 @@
         if d:
             ws[d] = (own[zd(d), :, AB:] + cr[zd(d), :, AB:]).astype(BF)
             send(ws.at[d], wr.at[d], wsem, (d,), dev_z(d), to=(0,))
-        for e in range(1, NX):
+        for e in far_first(NX):
             xs[d, e] = (own[zd(d), xd(e), :AB] + cr[zd(d), xd(e), :AB]).astype(BF)
             send(xs.at[d, e], xr.at[d, e], xsem, (d, e), dev_x(e), to=(d, 0))
     for d in order:
@@ -180,7 +182,7 @@
     for d in range(1, NZ):
         acc = acc + wr[d].astype(F32)
     own[z, :, AB:] = acc
-    for e in range(1, NX):
+    for e in far_first(NX):
         ts[e] = own[z, xd(e), AB:].astype(BF)
         send(ts.at[e], tr.at[e], tsem, (e,), dev_x(e), to=(0,))
 
@@ -244,7 +246,7 @@
         else:
             gb[0, 0, s - HA] = v
 
-    for e in range(1, NX):
+    for e in far_first(NX):
         send(ga.at[0, 0], ga.at[0, e], agx, (e,), dev_x(e))
     for i in range(1, NZ):
         send(gb.at[0, 0], gb.at[0, i], agz, (i,), dev_z(near(i)))
@@ -336,7 +338,7 @@
         if d:
             w5s[d] = p5f[d, :, RA:].astype(BF)
             send(w5s.at[d], w5r.at[d], w5sem, (d,), dev_z(d), to=(0,))
-        for e in range(1, NX):
+        for e in far_first(NX):
             p5s[d, e] = p5f[d, xd(e), :RA].astype(BF)
             send(p5s.at[d, e], p5r.at[d, e], p5sem, (d, e), dev_x(e), to=(d, 0))
     for d in order:
@@ -353,7 +355,7 @@
     for d in range(1, NZ):
         acc = acc + w5r[d].astype(F32)
     p5f[0, :, RA:] = acc
-    for e in range(1, NX):
+    for e in far_first(NX):
         t5s[e] = p5f[0, xd(e), RA:].astype(BF)
         send(t5s.at[e], t5r.at[e], t5sem, (e,), dev_x(e), to=(0,))
     drain()
@@ -456,7 +458,7 @@
     both = pl.pallas_call(
         body,
         name="backward",
-        out_shape=jax.ShapeDtypeStruct((sz.TO + sz.TC, sz.C), BF),
+        out_shape=pltpu.VMEM((sz.TO + sz.TC, sz.C), BF),
         in_specs=[hbm] * 7,
         out_specs=vmem,
         scratch_shapes=list(scratch.values()),

time: 76.3 us -> 74.1 us (0.971)
  the two profiles are of different devices: /device:TPU:8 before, /device:TPU:2 now
where the time goes in v3:
time: 74.1 us; the launch traced here: 74 us
  Pallas kernels  72.8 us (98%)
    pallas_call x1, Pallas kernels, per_device(): pl.pallas_call(body, name='backward', out_shape=pltpu.VMEM((sz.TO + sz.TC...  72.8 us

profile of v3, /device:TPU:2, one launch (start us, length us, event | category | flops | bytes accessed | tf_op | source)
XLA Modules:
  0.0 74.0 jit_solution(9758709065006136801)
XLA Ops:
  0.6 72.8 %backward.1 = bf16[80,256]{1,0:T(8,128)(2,1)S(1)} custom-call(bf16[320,256]{1,0:T(8,128)(2,1)} %refs_0_.1, bf16[320,2560]{1,0:T(8,128)(2,1)} %refs_1_.1, bf16[1,320,256]{2,1,0:T(8,128)(2,1)} %refs_2_.1, bf16[1,320,1280]{2,1,0:T(8,128)(2,1)} %refs_3_.1, bf16[1,320,2560]{2,1,0:T(8,128)(2,1)} %bitcast.3, s32[2,160]{1,0:T(2,128)} %refs_5_.1, s32[2]{0:T(128)} %refs_6_.1), custom_call_target="tpu_custom_call" | custom-call | tf_op jit(solution)/shard_map/backward/pallas_call | solution.py:458
  73.4 0.6 slice_bitcast_fusion

commit v4 on v3

--- a/solution.py
+++ b/solution.py
@@ -28,7 +28,7 @@
         self.U = coupling.shape[1]
         self.G = self.U // BLOCK
         self.HA = max(self.G // 5, 1)
-        self.CY = self.C // self.NY
+        self.SY = self.S3 // self.NY
         self.TO = self.T1 // (2 * self.Q)
         self.TC = self.T3 // self.Q
         self.TZ = self.T1 // self.NZ
@@ -37,24 +37,6 @@
         starts = [self.TZ * z // BLOCK for z in range(self.NZ)]
         ends = [-(-self.TZ * (z + 1) // BLOCK) for z in range(self.NZ)]
         self.SPAN = max(e - s for s, e in zip(starts, ends))
-        self.full = self.S3 // BLOCK
-        self.packed = (self.CY * self.S3 // BLOCK, BLOCK)
-
-    def pack(self, v):
-        h = self.CY // 2
-        parts = [v[:, i * BLOCK:(i + 1) * BLOCK] for i in range(self.full)]
-        if self.S3 % BLOCK:
-            rest = v[:, self.full * BLOCK:]
-            parts.append(jnp.concatenate([rest[:h], rest[h:]], axis=1))
-        return jnp.concatenate(parts, axis=0)
-
-    def unpack(self, v):
-        h, n = self.CY // 2, self.CY
-        parts = [v[i * n:(i + 1) * n] for i in range(self.full)]
-        if self.S3 % BLOCK:
-            rest = v[self.full * n:]
-            parts.append(jnp.concatenate([rest[:, :BLOCK // 2], rest[:, BLOCK // 2:]], axis=0))
-        return jnp.concatenate(parts, axis=1)
 
 
 def far_first(n):
@@ -63,8 +45,8 @@
 
 def kernel(
     sz, rrhs, rinv, crhs, cinv, coup, bmap, bcnt, out, *,
-    rrhs_v, rinv_v, crhs_v, coup_v, cinv_v, bmap_s, bcnt_s, cit, rhs_t, crhs_t, cs, cr, own, xs, xr, zs, zr, ws, wr, ts, tr, sol,
-    ysd, yrc, ga, gb, lhs, ycs, y1s, ycr, red, red_s, o1, o2, ot, p5f, p5s, p5r, z5s, z5r, w5s, w5r, t5s, t5r, sel, pos,
+    rrhs_v, rinv_v, crhs_v, coup_v, cinv_v, bmap_s, bcnt_s, cit, rhs_t, crhs_f, cs, cr, own, xs, xr, zs, zr, ws, wr, ts, tr, sol,
+    ysd, yrc, ga, gb, lhs, ycs, y1s, ycr, red, o1, o2, ot, p5f, p5s, p5r, z5s, z5r, w5s, w5r, t5s, t5r, sel, pos,
     lsem, csem, xsem, zsem, wsem, tsem, c2sem, ysem, o1sem, o2sem, agx, aga, agz, agc, y1sem, y2sem, p5sem, z5sem, w5sem, t5sem,
 ):
     NX, NZ, NY, HB, NB, G, HA = sz.NX, sz.NZ, sz.NY, sz.HB, sz.NB, sz.G, sz.HA
@@ -265,18 +247,21 @@
         spread(i)
     load_coup.wait()
 
+    def place(i, e):
+        q = zd(-near(i)) * NX + xd(-e)
+        for s in range(G):
+            lhs[q, :, s * BLOCK:(s + 1) * BLOCK] = ga[i, e, s] if s < HA else gb[e, i, s - HA]
+
     for i in range(1, NZ):
         arrived(ga.at[i], aga, (i,))
-    for s in range(HA):
-        lhs[:, s * BLOCK:(s + 1) * BLOCK] = ga[:, :, s].reshape(sz.C, BLOCK)
-    for e in range(1, NX):
-        arrived(gb.at[e], agc, (e, 0))
-    for s in range(HA, G):
-        v = jnp.stack([gb[e, :, s - HA] for e in range(NX)], axis=1)
-        lhs[:, s * BLOCK:(s + 1) * BLOCK] = v.reshape(sz.C, BLOCK)
-    prod = lax.dot_general(lhs[...], coup_v[...], (((1,), (1,)), ((), ())), preferred_element_type=F32)
-    for t in range(NY):
-        ycs[t] = sz.pack(prod[t * sz.CY:(t + 1) * sz.CY, :])
+    for e in range(NX):
+        if e:
+            arrived(gb.at[e], agc, (e, 0))
+        for i in range(NZ):
+            place(i, e)
+    prod = lax.dot_general(
+        coup_v[...], lhs[...].reshape(sz.C, sz.U), (((1,), (1,)), ((), ())), preferred_element_type=F32)
+    ycs[...] = prod.reshape(NY, sz.SY, sz.C)
     for d in far_first(NY):
         y1s[d] = ycs[yd(d)].astype(BF)
         send(y1s.at[d], ycr.at[d], y1sem, (d,), dev_y(d))
@@ -289,7 +274,7 @@
     o1[z] = sol[pl.ds(first_block(z), sz.SPAN)]
 
     load_crhs.wait()
-    crhs_t[...] = crhs_v[...].astype(F32).T
+    crhs_f[...] = crhs_v[...].astype(F32).reshape(NY, sz.SY, sz.C)
     load_cinv.wait()
     for j in range(sz.T3 // BLOCK):
         cols = slice(j * BLOCK, (j + 1) * BLOCK)
@@ -299,15 +284,9 @@
     for d in far_first(NY)[::-1]:
         arrived(ycr.at[d], y1sem, (d,))
         acc = acc + ycr[d].astype(F32)
-    acc = sz.unpack(acc)
-    from_z = zd(-near(r))
-    diff = []
-    for e in range(NX):
-        rows = pl.ds(pl.multiple_of((from_z * NX + xd(-e)) * 8, 8), 8)
-        diff.append(crhs_t[rows, :] - acc[e * 8:(e + 1) * 8, :])
-    red[0] = sz.pack(jnp.concatenate(diff, axis=0)).astype(BF)
+    red[r] = (crhs_f[r] - acc).astype(BF)
     for d in far_first(NY):
-        send(red.at[0], red.at[d], y2sem, (d,), dev_y(d))
+        send(red.at[r], red.at[r], y2sem, (d,), dev_y(d))
 
     for d in range(1, NZ):
         arrived(o1.at[zd(-d)], o1sem, (d,))
@@ -324,16 +303,12 @@
     out[:sz.TO] = ot[pl.ds(pl.multiple_of(first_row, 8), sz.TO), :].astype(BF)
 
     for d in range(1, NY):
-        arrived(red.at[d], y2sem, (d,))
-    for d in range(NY):
-        v = sz.unpack(red[d].astype(F32)).astype(BF).reshape(NX, 8, sz.S3)
-        for e in range(NX):
-            red_s[zd(-near(yd(-d))), xd(-e)] = v[e]
-    reduced = red_s[...].reshape(sz.C, sz.S3)
+        arrived(red.at[yd(-d)], y2sem, (d,))
+    reduced = red[...].astype(F32).reshape(sz.S3, sz.C).astype(BF)
     rows_z = NX * sz.TC
     for d in order:
         rows = pl.ds(pl.multiple_of(zd(d) * rows_z, rows_z), rows_z)
-        v = lax.dot_general(cit[rows, :], reduced, (((1,), (1,)), ((), ())), preferred_element_type=F32)
+        v = jnp.dot(cit[rows, :], reduced, preferred_element_type=F32)
         p5f[d] = v.reshape(NX, sz.TC, sz.C)
         if d:
             w5s[d] = p5f[d, :, RA:].astype(BF)
@@ -392,7 +367,7 @@
         bcnt_s=pltpu.SMEM(block_count.shape, jnp.int32),
         cit=pltpu.VMEM((sz.T3, sz.S3), BF),
         rhs_t=pltpu.VMEM((sz.C, sz.S1), BF),
-        crhs_t=pltpu.VMEM((sz.C, sz.S3), F32),
+        crhs_f=pltpu.VMEM((NY, sz.SY, sz.C), F32),
         cs=pltpu.VMEM((NZ, NX, HB, 8, BLOCK), F32),
         cr=pltpu.VMEM((NZ, NX, HB, 8, BLOCK), F32),
         own=pltpu.VMEM((NZ, NX, HB, 8, BLOCK), F32),
@@ -409,12 +384,11 @@
         yrc=pltpu.VMEM((NY * CAP, 8, BLOCK), BF),
         ga=pltpu.VMEM((NZ, NX, HA, 8, BLOCK), BF),
         gb=pltpu.VMEM((NX, NZ, G - HA, 8, BLOCK), BF),
-        lhs=pltpu.VMEM((sz.C, sz.U), BF),
-        ycs=pltpu.VMEM((NY,) + sz.packed, F32),
-        y1s=pltpu.VMEM((NY,) + sz.packed, BF),
-        ycr=pltpu.VMEM((NY,) + sz.packed, BF),
-        red=pltpu.VMEM((NY,) + sz.packed, BF),
-        red_s=pltpu.VMEM((NZ, NX, 8, sz.S3), BF),
+        lhs=pltpu.VMEM((Q, 8, sz.U), BF),
+        ycs=pltpu.VMEM((NY, sz.SY, sz.C), F32),
+        y1s=pltpu.VMEM((NY, sz.SY, sz.C), BF),
+        ycr=pltpu.VMEM((NY, sz.SY, sz.C), BF),
+        red=pltpu.VMEM((NY, sz.SY, sz.C), BF),
         o1=pltpu.VMEM((NZ, sz.SPAN, 8, BLOCK), BF),
         o2=pltpu.VMEM((NX, NZ, sz.SPAN, 8, BLOCK), BF),
         ot=pltpu.VMEM((sz.SPAN * BLOCK, sz.C), F32),

time: 74.1 us -> 73.8 us (level)
  no operation moved by 1% of the time
where the time goes in v4:
time: 73.8 us; the launch traced here: 73.7 us
  Pallas kernels  72.4 us (98%)
    pallas_call x1, Pallas kernels, per_device(): pl.pallas_call(body, name='backward', out_shape=pltpu.VMEM((sz.TO + sz.TC...  72.4 us

profile of v4, /device:TPU:2, one launch (start us, length us, event | category | flops | bytes accessed | tf_op | source)
XLA Modules:
  0.0 73.7 jit_solution(5748315073058642868)
XLA Ops:
  0.6 72.4 %backward.1 = bf16[80,256]{1,0:T(8,128)(2,1)S(1)} custom-call(bf16[320,256]{1,0:T(8,128)(2,1)} %refs_0_.1, bf16[320,2560]{1,0:T(8,128)(2,1)} %refs_1_.1, bf16[1,320,256]{2,1,0:T(8,128)(2,1)} %refs_2_.1, bf16[1,320,1280]{2,1,0:T(8,128)(2,1)} %refs_3_.1, bf16[1,320,2560]{2,1,0:T(8,128)(2,1)} %bitcast.3, s32[2,160]{1,0:T(2,128)} %refs_5_.1, s32[2]{0:T(128)} %refs_6_.1), custom_call_target="tpu_custom_call" | custom-call | tf_op jit(solution)/shard_map/backward/pallas_call | solution.py:432
  73.1 0.6 slice_bitcast_fusion

commit v5 on v4

--- a/solution.py
+++ b/solution.py
@@ -247,21 +247,30 @@
         spread(i)
     load_coup.wait()
 
-    def place(i, e):
+    def place(lo, hi, i, e):
         q = zd(-near(i)) * NX + xd(-e)
-        for s in range(G):
+        for s in range(lo, hi):
             lhs[q, :, s * BLOCK:(s + 1) * BLOCK] = ga[i, e, s] if s < HA else gb[e, i, s - HA]
 
-    for i in range(1, NZ):
-        arrived(ga.at[i], aga, (i,))
-    for e in range(NX):
-        if e:
-            arrived(gb.at[e], agc, (e, 0))
+    def product(lo, hi):
+        cols = slice(lo * BLOCK, hi * BLOCK)
+        return lax.dot_general(
+            coup_v[:, cols], lhs[:, :, cols].reshape(sz.C, (hi - lo) * BLOCK), (((1,), (1,)), ((), ())),
+            preferred_element_type=F32)
+
+    for i in range(NZ):
+        if i:
+            arrived(ga.at[i], aga, (i,))
+        for e in range(NX):
+            place(0, HA, i, e)
+        place(HA, G, i, 0)
+    ycs[...] = product(0, HA).reshape(NY, sz.SY, sz.C)
+    for e in range(1, NX):
+        arrived(gb.at[e], agc, (e, 0))
         for i in range(NZ):
-            place(i, e)
-    prod = lax.dot_general(
-        coup_v[...], lhs[...].reshape(sz.C, sz.U), (((1,), (1,)), ((), ())), preferred_element_type=F32)
-    ycs[...] = prod.reshape(NY, sz.SY, sz.C)
+            place(HA, G, i, e)
+    prod = product(HA, G)
+    ycs[...] = ycs[...] + prod.reshape(NY, sz.SY, sz.C)
     for d in far_first(NY):
         y1s[d] = ycs[yd(d)].astype(BF)
         send(y1s.at[d], ycr.at[d], y1sem, (d,), dev_y(d))

time: 73.8 us -> 74.2 us (level)
  the two profiles are of different devices: /device:TPU:2 before, /device:TPU:64 now
where the time goes in v5:
time: 74.2 us; the launch traced here: 74.1 us
  Pallas kernels  72.8 us (98%)
    pallas_call x1, Pallas kernels, per_device(): pl.pallas_call(body, name='backward', out_shape=pltpu.VMEM((sz.TO + sz.TC...  72.8 us

profile of v5, /device:TPU:64, one launch (start us, length us, event | category | flops | bytes accessed | tf_op | source)
XLA Modules:
  0.0 74.1 jit_solution(13792873870074175939)
XLA Ops:
  0.6 72.8 %backward.1 = bf16[80,256]{1,0:T(8,128)(2,1)S(1)} custom-call(bf16[320,256]{1,0:T(8,128)(2,1)} %refs_0_.1, bf16[320,2560]{1,0:T(8,128)(2,1)} %refs_1_.1, bf16[1,320,256]{2,1,0:T(8,128)(2,1)} %refs_2_.1, bf16[1,320,1280]{2,1,0:T(8,128)(2,1)} %refs_3_.1, bf16[1,320,2560]{2,1,0:T(8,128)(2,1)} %bitcast.3, s32[2,160]{1,0:T(2,128)} %refs_5_.1, s32[2]{0:T(128)} %refs_6_.1), custom_call_target="tpu_custom_call" | custom-call | tf_op jit(solution)/shard_map/backward/pallas_call | solution.py:441
  73.5 0.6 slice_bitcast_fusion
